TPU v7x, 128 devices: a whole 4x4x4 slice. The times are simulated.
128 devices in a mesh: row: 8 (over x_hi, y), col: 16 (over z, x_lo, core).
Axes of the slice: x: 4 (x_hi: 2, x_lo: 2; x = x_hi * 2 + x_lo), y: 4, z: 4, core: 2. Of those that a mesh axis runs over, the one named last changes fastest.
Arguments:
- embeds: bfloat16 [2, 192, 16384], P(None, None, 'col'), may hold values from -40 to 40
- attn_gain: bfloat16 [16384], P('col'), may hold values from 0.099609375 to 1.8984375
- ffn_gain: bfloat16 [16384], P('col'), may hold values from 0.099609375 to 1.8984375
- query_weight: bfloat16 [16384, 16384], P(None, ('row', 'col')), may hold values from -0.046875 to 0.046875
- key_matrix: bfloat16 [16384, 1024], P(None, ('row', 'col')), may hold values from -0.046875 to 0.046875
- value_matrix: bfloat16 [16384, 1024], P(None, ('row', 'col')), may hold values from -0.046875 to 0.046875
- output_weight: bfloat16 [16384, 16384], P(('row', 'col')), may hold values from -0.046875 to 0.046875
- gate_weight: bfloat16 [16384, 13312], P(None, ('row', 'col')), may hold values from -0.046875 to 0.046875
- up_weight: bfloat16 [16384, 13312], P(None, ('row', 'col')), may hold values from -0.046875 to 0.046875
- down_weight: bfloat16 [13312, 16384], P(('row', 'col')), may hold values from -0.0546875 to 0.0546875
- rotated_key_cache: bfloat16 [192, 8, 1024, 128], P('col', 'row'), may hold values from -400 to 400
- stored_value_cache: bfloat16 [192, 8, 1024, 128], P('col', 'row'), may hold values from -6 to 6
- lengths: int32 [192], P('col'), may hold values from 2 to 1024, as said below
- positions: int32 [192], P('col'), may hold values from 0 to 8191
Outputs:
- layer_out: bfloat16 [2, 192, 16384], P(None, None, 'col')
- appended: bfloat16 [2, 192, 2, 1024], P(None, 'col', None, 'row')
Inputs may be any that keep to these rules, and one draw needn't show every extreme that they name: `lengths`: every draw has a row with all 1024 slots filled and a row with 2.
All inputs are finite; a program needn't handle non-finite values.
Results may differ from a plain program's by a relative error of at most 0.0075.
Values may be sent and summed in bfloat16 or wider, within the bound.
A program may use at most 192 MiB of HBM per device.

v0:
```python
import math

import jax
import jax.numpy as jnp
from jax import lax
from jax.sharding import PartitionSpec as P

MODEL_WIDTH = 16384
QUERY_HEADS = 128
KEY_HEADS = 8
HEAD_WIDTH = 128
STEPS = 2
CACHE_SLOTS = 1024


EPS = 1e-05
THETA = 500000.0


def rope_tables(positions, head_size):
    half_size = head_size // 2
    frequency = THETA ** (-2.0 * jnp.arange(half_size, dtype=jnp.float32) / head_size)
    angles = positions.astype(jnp.float32)[:, None] * frequency[None, :]
    return (jnp.cos(angles), jnp.sin(angles))


def apply_rotation(value_tensor, cosine_table, sine_table):
    half_size = value_tensor.shape[-1] // 2
    leading = value_tensor[..., :half_size]
    trailing = value_tensor[..., half_size:]
    cosine_table = cosine_table[:, None, :]
    sine_table = sine_table[:, None, :]
    return jnp.concatenate(
        [
            leading * cosine_table - trailing * sine_table,
            trailing * cosine_table + leading * sine_table,
        ],
        axis=-1,
    )


def attend_cache(
    query_tensor, rotated_key_cache, stored_value_cache, valid_mask, new_keys, new_values
):
    factor = 1.0 / math.sqrt(query_tensor.shape[-1])
    cached = (
        jnp.einsum(
            "bgqd,bgjd->bgqj", query_tensor, rotated_key_cache, preferred_element_type=jnp.float32
        )
        * factor
    )
    recent = (
        jnp.einsum("bgqd,bgtd->bgqt", query_tensor, new_keys, preferred_element_type=jnp.float32)
        * factor
    )
    usable = valid_mask[:, None, None, :]
    highest = jnp.maximum(
        jnp.max(jnp.where(usable, cached, -jnp.inf), axis=-1), jnp.max(recent, axis=-1)
    )[..., None]
    cached_weight = jnp.where(usable, jnp.exp(cached - highest), 0.0)
    recent_weight = jnp.exp(recent - highest)
    denominator = jnp.sum(cached_weight, axis=-1, keepdims=True) + jnp.sum(
        recent_weight, axis=-1, keepdims=True
    )
    cached_prob = (cached_weight / denominator).astype(jnp.bfloat16)
    recent_prob = (recent_weight / denominator).astype(jnp.bfloat16)
    blended = jnp.einsum(
        "bgqj,bgjd->bgqd", cached_prob, stored_value_cache, preferred_element_type=jnp.float32
    )
    blended = blended + jnp.einsum(
        "bgqt,bgtd->bgqd", recent_prob, new_values, preferred_element_type=jnp.float32
    )
    return blended.astype(jnp.bfloat16)


def block_norm(value_tensor, gain):
    widened = value_tensor.astype(jnp.float32)
    squares = lax.psum(jnp.sum(widened * widened, axis=-1, keepdims=True), "col")
    return (widened * lax.rsqrt(squares / MODEL_WIDTH + EPS) * gain.astype(jnp.float32)).astype(
        jnp.bfloat16
    )


def row_total(partial_value):
    return lax.psum(partial_value, "row")


def gated(gate, upper):
    return (jax.nn.silu(gate) * upper).astype(jnp.bfloat16)


def on_device(
    embeds,
    attn_gain,
    ffn_gain,
    query_weight,
    key_matrix,
    value_matrix,
    output_weight,
    gate_weight,
    up_weight,
    down_weight,
    rotated_key_cache,
    stored_value_cache,
    lengths,
    positions,
):
    local_rows = rotated_key_cache.shape[0]
    local_heads = rotated_key_cache.shape[1]
    queries_per_group = QUERY_HEADS // KEY_HEADS
    valid_mask = jnp.arange(CACHE_SLOTS, dtype=jnp.int32)[None, :] < lengths[:, None]
    latest_keys = []
    latest_values = []
    outputs = []
    appended = []

    def attention(query_rows, key_rows, value_rows, step):
        cosine_table, sine_table = rope_tables(positions + step, HEAD_WIDTH)
        query_tensor = apply_rotation(
            query_rows.reshape(local_rows, local_heads * queries_per_group, HEAD_WIDTH),
            cosine_table,
            sine_table,
        ).astype(jnp.bfloat16)
        key_tensor = apply_rotation(
            key_rows.reshape(local_rows, local_heads, HEAD_WIDTH), cosine_table, sine_table
        ).astype(jnp.bfloat16)
        value_tensor = value_rows.reshape(local_rows, local_heads, HEAD_WIDTH).astype(jnp.bfloat16)
        latest_keys.append(key_tensor)
        latest_values.append(value_tensor)
        appended.append(
            jnp.stack(
                [
                    key_tensor.reshape(local_rows, local_heads * HEAD_WIDTH),
                    value_tensor.reshape(local_rows, local_heads * HEAD_WIDTH),
                ],
                axis=1,
            )
        )
        head_count = attend_cache(
            query_tensor.reshape(local_rows, local_heads, queries_per_group, HEAD_WIDTH),
            rotated_key_cache,
            stored_value_cache,
            valid_mask,
            jnp.stack(latest_keys, axis=2),
            jnp.stack(latest_values, axis=2),
        )
        return head_count.reshape(local_rows, local_heads * queries_per_group * HEAD_WIDTH)

    query_block, key_block, value_block, gate_block, upper_block = (
        lax.all_to_all(query_weight, "col", split_axis=0, concat_axis=1, tiled=True),
        lax.all_to_all(key_matrix, "col", split_axis=0, concat_axis=1, tiled=True),
        lax.all_to_all(value_matrix, "col", split_axis=0, concat_axis=1, tiled=True),
        lax.all_to_all(gate_weight, "col", split_axis=0, concat_axis=1, tiled=True),
        lax.all_to_all(up_weight, "col", split_axis=0, concat_axis=1, tiled=True),
    )
    output_block, down_block = (
        lax.all_to_all(output_weight, "col", split_axis=1, concat_axis=0, tiled=True),
        lax.all_to_all(down_weight, "col", split_axis=1, concat_axis=0, tiled=True),
    )
    for step in range(STEPS):
        current = embeds[step]
        normed = block_norm(current, attn_gain)
        query_part = jnp.dot(normed, query_block, preferred_element_type=jnp.float32)
        key_part = jnp.dot(normed, key_block, preferred_element_type=jnp.float32)
        value_part = jnp.dot(normed, value_block, preferred_element_type=jnp.float32)
        query_rows, key_rows, value_rows = (
            lax.psum_scatter(query_part, "col", scatter_dimension=0, tiled=True),
            lax.psum_scatter(key_part, "col", scatter_dimension=0, tiled=True),
            lax.psum_scatter(value_part, "col", scatter_dimension=0, tiled=True),
        )
        head_count = attention(query_rows, key_rows, value_rows, step)
        attn_part = jnp.dot(
            lax.all_gather(head_count, "col", axis=0, tiled=True),
            output_block,
            preferred_element_type=jnp.float32,
        )
        residual = (current.astype(jnp.float32) + row_total(attn_part)).astype(jnp.bfloat16)
        normed_ffn = block_norm(residual, ffn_gain)
        gate_part = jnp.dot(normed_ffn, gate_block, preferred_element_type=jnp.float32)
        upper_part = jnp.dot(normed_ffn, upper_block, preferred_element_type=jnp.float32)
        gate, upper = lax.psum((gate_part, upper_part), "col")
        hidden = gated(gate, upper)
        down_part = jnp.dot(hidden, down_block, preferred_element_type=jnp.float32)
        outputs.append((residual.astype(jnp.float32) + row_total(down_part)).astype(jnp.bfloat16))
    return (jnp.stack(outputs), jnp.stack(appended))


def solution(mesh):
    in_specs = (
        P(None, None, "col"),
        P("col"),
        P("col"),
        P(None, ("row", "col")),
        P(None, ("row", "col")),
        P(None, ("row", "col")),
        P(("row", "col"), None),
        P(None, ("row", "col")),
        P(None, ("row", "col")),
        P(("row", "col"), None),
        P("col", "row", None, None),
        P("col", "row", None, None),
        P("col"),
        P("col"),
    )
    out_specs = (P(None, None, "col"), P(None, "col", None, "row"))
    return jax.shard_map(
        on_device, mesh=mesh, in_specs=in_specs, out_specs=out_specs, check_vma=False
    )
```

profile of v0, /device:TPU:0, one launch (start us, length us, event | category | flops | bytes accessed | tf_op | source)
XLA Modules:
  0.0 844.8 jit_solution(7521457974809017112)
XLA Ops:
  7.2 14.9 %all_to_all.133 = bf16[16,1024,8]{1,2,0:T(8,128)(2,1)} all-to-all(bf16[16,1024,8]{1,2,0:T(8,128)(2,1)} %bitcast.211), channel_id=1, replica_groups=mesh['row'=8,'col'=16] {'col'}, dimensions={0} | all-to-all | bytes 524288 | tf_op jit(solution)/shard_map/all_to_all | solution.py:152
  22.0 11.5 %all_to_all.134 = bf16[16,1024,8]{1,2,0:T(8,128)(2,1)S(1)} all-to-all(bf16[16,1024,8]{1,2,0:T(8,128)(2,1)} %bitcast.212), channel_id=1, replica_groups=mesh['row'=8,'col'=16] {'col'}, dimensions={0} | all-to-all | bytes 524288 | tf_op jit(solution)/shard_map/all_to_all | solution.py:151
  33.6 4.7 all-to-all-start
  38.3 6.4 copy.98
  46.0 64.2 %all-reduce.13 = (f32[192,1]{0,1:T(1,128)S(1)}, f32[192,1]{0,1:T(1,128)S(1)}) all-reduce(f32[192,1]{0,1:T(1,128)S(1)} %bitcast.228, f32[192,1]{0,1:T(1,128)S(1)} %bitcast.227), channel_id=1, replica_groups=mesh['row'=8,'col'=16] {'col'}, use_global_device_ids=true, to_apply=%region_14.15 | all-reduce | flops 384 | bytes 3072 | tf_op jit(solution)/shard_map/psum | solution.py:78
  111.6 4.5 all-to-all-start.3
  122.5 6.4 copy.97
  128.9 5.1 fusion.138
  136.7 78.2 %fusion.144 = (f32[16,2048]{1,0:T(8,128)S(1)}, f32[16,128]{1,0:T(8,128)}, f32[16,128]{1,0:T(8,128)}, f32[16,128]{1,0:T(8,128)S(1)}, f32[16,128]{1,0:T(8,128)S(1)}, /*index=5*/f32[16,2048]{1,0:T(8,128)S(1)}) fusion(f32[192,2048]{1,0:T(8,128)} %fusion.142, f32[192,128]{1,0:T(8,128)} %fusion.74, f32[192,128]{1,0:T(8,128)} %fusion.76, ...), kind=kCustom, calls=%all-reduce-scatter.6 | all-reduce-scatter fusion | flops 1179649 | bytes 3834368
  220.5 4.6 collective-permute-start.11
  238.2 4.5 all-to-all-start.4
  242.8 6.4 copy.99
  263.6 11.8 %collective-permute-done.23 = bf16[12,128]{1,0:T(8,128)(2,1)S(1)} collective-permute-done((bf16[12,128]{1,0:T(8,128)(2,1)S(1)}, bf16[12,128]{1,0:T(8,128)(2,1)S(1)}, u32[]{:S(2)}, u32[]{:S(2)}) %collective-permute-start.23) | collective-permute-done | bytes 3104
  275.4 9.1 %collective-permute-start.17 = (f32[16,128]{1,0:T(8,128)}, f32[16,128]{1,0:T(8,128)}, u32[]{:S(2)}, u32[]{:S(2)}) collective-permute-start(f32[16,128]{1,0:T(8,128)} %get-tuple-element.45), channel_id=1, source_target_pairs={{0,2},{1,3},{2,4},{3,5},{4,6},{5,7},{6,8},{7,9},{8,10},{9,11},{10,... | collective-permute-start | bytes 24584
  286.4 5.1 collective-permute-start.4
  298.3 5.1 collective-permute-start.6
  308.2 6.7 concatenate.91
  326.1 6.7 concatenate.88
  344.4 8.1 concatenate.87
  353.6 8.2 concatenate.90
  367.7 22.4 %all-gather = bf16[16,12,2048]{2,1,0:T(8,128)(2,1)S(1)} all-gather(bf16[1,12,2048]{2,1,0:T(8,128)(2,1)S(1)} %reshape.632), channel_id=1, replica_groups=mesh['row'=8,'col'=16] {'col'}, dimensions={0}, use_global_device_ids=true | all-gather | bytes 835584 | tf_op jit(solution)/shard_map/all_gather | solution.py:173
  393.7 21.8 %all-gather.1 = bf16[16,12,2048]{2,1,0:T(8,128)(2,1)S(1)} all-gather(bf16[1,12,2048]{2,1,0:T(8,128)(2,1)S(1)} %reshape.634), channel_id=1, replica_groups=mesh['row'=8,'col'=16] {'col'}, dimensions={0}, use_global_device_ids=true | all-gather | bytes 835584 | tf_op jit(solution)/shard_map/all_gather | solution.py:173
  415.7 4.5 all-to-all-start.5
  426.6 97.3 %all-reduce.26.cloned.1.call-done = (f32[192,1024]{1,0:T(8,128)}, f32[192,1024]{1,0:T(8,128)}) async-done(((f32[192,1024]{1,0:T(8,128)}, f32[192,1024]{1,0:T(8,128)}), (f32[192,1024]{1,0:T(8,128)}, f32[192,1024]{1,0:T(8,128)})) %all-reduce.26.cloned.1.call-update) | async-done | bytes 1572880 | tf_op jit(solution)/shard_map/psum | solution.py:85
  525.5 27.2 %all-reduce.12 = (f32[192,1]{0,1:T(1,128)S(1)}, f32[192,1]{0,1:T(1,128)S(1)}) all-reduce(f32[192,1]{0,1:T(1,128)S(1)} %bitcast.226, f32[192,1]{0,1:T(1,128)S(1)} %bitcast.225), channel_id=1, replica_groups=mesh['row'=8,'col'=16] {'col'}, use_global_device_ids=true, to_apply=%region_24.25 | all-reduce | flops 384 | bytes 3072 | tf_op jit(solution)/shard_map/psum | solution.py:78
  557.1 4.3 fusion.82
  561.5 4.4 fusion.80
  565.9 4.4 fusion.78
  572.7 81.9 %all_to_all.135 = bf16[104,16,1024]{2,0,1:T(8,128)(2,1)} all-to-all(bf16[104,16,1024]{2,0,1:T(8,128)(2,1)S(1)} %bitcast.200), channel_id=1, replica_groups=mesh['row'=8,'col'=16] {'col'}, dimensions={1} | all-to-all | bytes 6815744 | tf_op jit(solution)/shard_map/all_to_all | solution.py:158
  654.7 83.7 %all-reduce.22.cloned.1.call-done = (f32[192,1664]{1,0:T(8,128)}, f32[192,1664]{1,0:T(8,128)}, f32[192,1664]{1,0:T(8,128)}, f32[192,1664]{1,0:T(8,128)}) async-done(((f32[192,1664]{1,0:T(8,128)}, f32[192,1664]{1,0:T(8,128)}, f32[192,1664]{1,0:T(8,128)}, f32[192,1664]{1,0:T(8,128)}), (f32[192,1664]{1,0:T(8,128)}, f32[192,1664]{1,0:T(8,128)}, f32[192,1664]{1,0:T(8,128)}, ...) | async-done | bytes 5111824 | tf_op jit(solution)/shard_map/psum | solution.py:181
  738.3 4.8 fusion.54
  746.7 88.0 %all-reduce.24.cloned.1.call-done = (f32[192,1024]{1,0:T(8,128)}, f32[192,1024]{1,0:T(8,128)}) async-done(((f32[192,1024]{1,0:T(8,128)}, f32[192,1024]{1,0:T(8,128)}), (f32[192,1024]{1,0:T(8,128)}, f32[192,1024]{1,0:T(8,128)})) %all-reduce.24.cloned.1.call-update) | async-done | bytes 1572880 | tf_op jit(solution)/shard_map/psum | solution.py:85
  (217 shorter events, 112.5 us)
Async XLA Ops:
  7.2 356.4 %copy-start = (bf16[12,1,1024,128]{3,2,1,0:T(8,128)(2,1)S(1)}, bf16[12,1,1024,128]{3,2,1,0:T(8,128)(2,1)}, u32[]{:S(2)}) copy-start(bf16[12,1,1024,128]{3,2,1,0:T(8,128)(2,1)} %param.24) | copy-start | bytes 9437188
  33.6 78.0 %all-to-all-start = ((bf16[16,1024,128]{2,1,0:T(8,128)(2,1)}), bf16[16,1024,128]{2,1,0:T(8,128)(2,1)}, u32[]{:S(2)}, u32[]{:S(2)}) async-start(bf16[16,1024,128]{2,1,0:T(8,128)(2,1)} %bitcast.201), calls=%async_computation | async-start | bytes 8388608 | tf_op jit(solution)/shard_map/all_to_all | solution.py:150
  111.6 126.7 %all-to-all-start.3 = ((bf16[128,16,1024]{0,2,1:T(8,128)(2,1)}), bf16[128,16,1024]{0,2,1:T(8,128)(2,1)}, u32[]{:S(2)}, u32[]{:S(2)}) async-start(bf16[128,16,1024]{0,2,1:T(8,128)(2,1)} %bitcast.197), calls=%async_computation.3 | async-start | bytes 8388608 | tf_op jit(solution)/shard_map/all_to_all | solution.py:157
  214.9 37.5 %collective-permute-start.10 = (bf16[16,128]{1,0:T(8,128)(2,1)S(1)}, bf16[16,128]{1,0:T(8,128)(2,1)S(1)}, u32[]{:S(2)}, u32[]{:S(2)}) collective-permute-start(bf16[16,128]{1,0:T(8,128)(2,1)S(1)} %convert.76), channel_id=1, source_target_pairs={{0,3},{1,4},{2,5},{3,6},{4,7},{5,8},{6,9},{7,10},{8,11},{9,12},{10... | collective-permute-start | bytes 12296
  216.1 38.8 %collective-permute-start.8 = (bf16[16,128]{1,0:T(8,128)(2,1)S(1)}, bf16[16,128]{1,0:T(8,128)(2,1)S(1)}, u32[]{:S(2)}, u32[]{:S(2)}) collective-permute-start(bf16[16,128]{1,0:T(8,128)(2,1)S(1)} %convert.76), channel_id=1, source_target_pairs={{0,1},{1,2},{2,3},{3,4},{4,5},{5,6},{6,7},{7,8},{8,9},{9,10},{10,1... | collective-permute-start | bytes 12296
  218.7 40.4 %collective-permute-start.9 = (bf16[16,128]{1,0:T(8,128)(2,1)S(1)}, bf16[16,128]{1,0:T(8,128)(2,1)S(1)}, u32[]{:S(2)}, u32[]{:S(2)}) collective-permute-start(bf16[16,128]{1,0:T(8,128)(2,1)S(1)} %convert.76), channel_id=1, source_target_pairs={{0,2},{1,3},{2,4},{3,5},{4,6},{5,7},{6,8},{7,9},{8,10},{9,11},{10,... | collective-permute-start | bytes 12296
  220.5 28.7 %collective-permute-start.11 = (bf16[12,128]{1,0:T(8,128)(2,1)S(1)}, bf16[12,128]{1,0:T(8,128)(2,1)S(1)}, u32[]{:S(2)}, u32[]{:S(2)}) collective-permute-start(bf16[12,128]{1,0:T(8,128)(2,1)S(1)} %slice.50), channel_id=1, source_target_pairs={{0,4},{1,5},{2,6},{3,7},{4,8},{5,9},{6,10},{7,11},{8,12},{9,13},{1... | collective-permute-start | bytes 9224
  233.5 64.8 %collective-permute-start.16 = (f32[16,128]{1,0:T(8,128)}, f32[16,128]{1,0:T(8,128)S(1)}, u32[]{:S(2)}, u32[]{:S(2)}) collective-permute-start(f32[16,128]{1,0:T(8,128)} %get-tuple-element.45), channel_id=1, source_target_pairs={{0,1},{1,2},{2,3},{3,4},{4,5},{5,6},{6,7},{7,8},{8,9},{9,10},{10,1... | collective-permute-start | bytes 24584
  238.2 177.5 %all-to-all-start.4 = ((bf16[16,1024,104]{1,2,0:T(8,128)(2,1)}), bf16[16,1024,104]{1,2,0:T(8,128)(2,1)}, u32[]{:S(2)}, u32[]{:S(2)}) async-start(bf16[16,1024,104]{1,2,0:T(8,128)(2,1)} %bitcast.199), calls=%async_computation.4 | async-start | bytes 6815744 | tf_op jit(solution)/shard_map/all_to_all | solution.py:153
  249.2 35.4 %collective-permute-start.20 = (bf16[16,128]{1,0:T(8,128)(2,1)S(1)}, bf16[16,128]{1,0:T(8,128)(2,1)S(1)}, u32[]{:S(2)}, u32[]{:S(2)}) collective-permute-start(bf16[16,128]{1,0:T(8,128)(2,1)S(1)} %convert.77), channel_id=1, source_target_pairs={{0,1},{1,2},{2,3},{3,4},{4,5},{5,6},{6,7},{7,8},{8,9},{9,10},{10,1... | collective-permute-start | bytes 12296
  252.4 34.0 %collective-permute-start.21 = (bf16[16,128]{1,0:T(8,128)(2,1)S(1)}, bf16[16,128]{1,0:T(8,128)(2,1)S(1)}, u32[]{:S(2)}, u32[]{:S(2)}) collective-permute-start(bf16[16,128]{1,0:T(8,128)(2,1)S(1)} %convert.77), channel_id=1, source_target_pairs={{0,2},{1,3},{2,4},{3,5},{4,6},{5,7},{6,8},{7,9},{8,10},{9,11},{10,... | collective-permute-start | bytes 12296
  254.9 36.6 %collective-permute-start.22 = (bf16[16,128]{1,0:T(8,128)(2,1)S(1)}, bf16[16,128]{1,0:T(8,128)(2,1)S(1)}, u32[]{:S(2)}, u32[]{:S(2)}) collective-permute-start(bf16[16,128]{1,0:T(8,128)(2,1)S(1)} %convert.77), channel_id=1, source_target_pairs={{0,3},{1,4},{2,5},{3,6},{4,7},{5,8},{6,9},{7,10},{8,11},{9,12},{10... | collective-permute-start | bytes 12296
  259.1 16.3 %collective-permute-start.23 = (bf16[12,128]{1,0:T(8,128)(2,1)S(1)}, bf16[12,128]{1,0:T(8,128)(2,1)S(1)}, u32[]{:S(2)}, u32[]{:S(2)}) collective-permute-start(bf16[12,128]{1,0:T(8,128)(2,1)S(1)} %slice.53), channel_id=1, source_target_pairs={{0,4},{1,5},{2,6},{3,7},{4,8},{5,9},{6,10},{7,11},{8,12},{9,13},{1... | collective-permute-start | bytes 9224
  275.4 28.1 %collective-permute-start.17 = (f32[16,128]{1,0:T(8,128)}, f32[16,128]{1,0:T(8,128)}, u32[]{:S(2)}, u32[]{:S(2)}) collective-permute-start(f32[16,128]{1,0:T(8,128)} %get-tuple-element.45), channel_id=1, source_target_pairs={{0,2},{1,3},{2,4},{3,5},{4,6},{5,7},{6,8},{7,9},{8,10},{9,11},{10,... | collective-permute-start | bytes 24584
  284.5 20.3 %collective-permute-start.18 = (f32[16,128]{1,0:T(8,128)}, f32[16,128]{1,0:T(8,128)}, u32[]{:S(2)}, u32[]{:S(2)}) collective-permute-start(f32[16,128]{1,0:T(8,128)} %get-tuple-element.45), channel_id=1, source_target_pairs={{0,3},{1,4},{2,5},{3,6},{4,7},{5,8},{6,9},{7,10},{8,11},{9,12},{10... | collective-permute-start | bytes 24584
  286.4 32.9 %collective-permute-start.4 = (f32[16,128]{1,0:T(8,128)}, f32[16,128]{1,0:T(8,128)}, u32[]{:S(2)}, u32[]{:S(2)}) collective-permute-start(f32[16,128]{1,0:T(8,128)} %get-tuple-element.46), channel_id=1, source_target_pairs={{0,1},{1,2},{2,3},{3,4},{4,5},{5,6},{6,7},{7,8},{8,9},{9,10},{10,1... | collective-permute-start | bytes 24584
  291.5 3.6 collective-permute-start.19
  295.1 26.4 %collective-permute-start.5 = (f32[16,128]{1,0:T(8,128)}, f32[16,128]{1,0:T(8,128)}, u32[]{:S(2)}, u32[]{:S(2)}) collective-permute-start(f32[16,128]{1,0:T(8,128)} %get-tuple-element.46), channel_id=1, source_target_pairs={{0,2},{1,3},{2,4},{3,5},{4,6},{5,7},{6,8},{7,9},{8,10},{9,11},{10,... | collective-permute-start | bytes 24584
  298.3 25.9 %collective-permute-start.6 = (f32[16,128]{1,0:T(8,128)}, f32[16,128]{1,0:T(8,128)}, u32[]{:S(2)}, u32[]{:S(2)}) collective-permute-start(f32[16,128]{1,0:T(8,128)} %get-tuple-element.46), channel_id=1, source_target_pairs={{0,3},{1,4},{2,5},{3,6},{4,7},{5,8},{6,9},{7,10},{8,11},{9,12},{10... | collective-permute-start | bytes 24584
  303.5 36.9 %collective-permute-start = (f32[16,2048]{1,0:T(8,128)S(1)}, f32[16,2048]{1,0:T(8,128)S(1)}, u32[]{:S(2)}, u32[]{:S(2)}) collective-permute-start(f32[16,2048]{1,0:T(8,128)S(1)} %get-tuple-element.49), channel_id=1, source_target_pairs={{0,1},{1,2},{2,3},{3,4},{4,5},{5,6},{6,7},{7,8},{8,9},{9,10},{10,1... | collective-permute-start | bytes 393224
  304.9 11.3 %collective-permute-start.7 = (f32[12,128]{1,0:T(8,128)}, f32[12,128]{1,0:T(8,128)}, u32[]{:S(2)}, u32[]{:S(2)}) collective-permute-start(f32[12,128]{1,0:T(8,128)} %slice.49), channel_id=1, source_target_pairs={{0,4},{1,5},{2,6},{3,7},{4,8},{5,9},{6,10},{7,11},{8,12},{9,13},{1... | collective-permute-start | bytes 18440
  316.2 26.3 %collective-permute-start.1 = (f32[16,2048]{1,0:T(8,128)S(1)}, f32[16,2048]{1,0:T(8,128)}, u32[]{:S(2)}, u32[]{:S(2)}) collective-permute-start(f32[16,2048]{1,0:T(8,128)S(1)} %get-tuple-element.49), channel_id=1, source_target_pairs={{0,2},{1,3},{2,4},{3,5},{4,6},{5,7},{6,8},{7,9},{8,10},{9,11},{10,... | collective-permute-start | bytes 393224
  319.3 25.1 %collective-permute-start.2 = (f32[16,2048]{1,0:T(8,128)S(1)}, f32[16,2048]{1,0:T(8,128)}, u32[]{:S(2)}, u32[]{:S(2)}) collective-permute-start(f32[16,2048]{1,0:T(8,128)S(1)} %get-tuple-element.49), channel_id=1, source_target_pairs={{0,3},{1,4},{2,5},{3,6},{4,7},{5,8},{6,9},{7,10},{8,11},{9,12},{10... | collective-permute-start | bytes 393224
  321.5 32.1 %collective-permute-start.12 = (f32[16,2048]{1,0:T(8,128)S(1)}, f32[16,2048]{1,0:T(8,128)}, u32[]{:S(2)}, u32[]{:S(2)}) collective-permute-start(f32[16,2048]{1,0:T(8,128)S(1)} %get-tuple-element.44), channel_id=1, source_target_pairs={{0,1},{1,2},{2,3},{3,4},{4,5},{5,6},{6,7},{7,8},{8,9},{9,10},{10,1... | collective-permute-start | bytes 393224
  324.2 13.4 %collective-permute-start.3 = (f32[12,2048]{1,0:T(8,128)}, f32[12,2048]{1,0:T(8,128)}, u32[]{:S(2)}, u32[]{:S(2)}) collective-permute-start(f32[12,2048]{1,0:T(8,128)} %slice.48), channel_id=1, source_target_pairs={{0,4},{1,5},{2,6},{3,7},{4,8},{5,9},{6,10},{7,11},{8,12},{9,13},{1... | collective-permute-start | bytes 294920
  337.6 16.0 %collective-permute-start.13 = (f32[16,2048]{1,0:T(8,128)S(1)}, f32[16,2048]{1,0:T(8,128)}, u32[]{:S(2)}, u32[]{:S(2)}) collective-permute-start(f32[16,2048]{1,0:T(8,128)S(1)} %get-tuple-element.44), channel_id=1, source_target_pairs={{0,2},{1,3},{2,4},{3,5},{4,6},{5,7},{6,8},{7,9},{8,10},{9,11},{10,... | collective-permute-start | bytes 393224
  340.3 13.3 %collective-permute-start.14 = (f32[16,2048]{1,0:T(8,128)S(1)}, f32[16,2048]{1,0:T(8,128)}, u32[]{:S(2)}, u32[]{:S(2)}) collective-permute-start(f32[16,2048]{1,0:T(8,128)S(1)} %get-tuple-element.44), channel_id=1, source_target_pairs={{0,3},{1,4},{2,5},{3,6},{4,7},{5,8},{6,9},{7,10},{8,11},{9,12},{10... | collective-permute-start | bytes 393224
  342.5 11.1 %collective-permute-start.15 = (f32[12,2048]{1,0:T(8,128)}, f32[12,2048]{1,0:T(8,128)}, u32[]{:S(2)}, u32[]{:S(2)}) collective-permute-start(f32[12,2048]{1,0:T(8,128)} %slice.51), channel_id=1, source_target_pairs={{0,4},{1,5},{2,6},{3,7},{4,8},{5,9},{6,10},{7,11},{8,12},{9,13},{1... | collective-permute-start | bytes 294920
  415.7 141.4 %all-to-all-start.5 = ((bf16[16,1024,104]{1,2,0:T(8,128)(2,1)}), bf16[16,1024,104]{1,2,0:T(8,128)(2,1)}, u32[]{:S(2)}, u32[]{:S(2)}) async-start(bf16[16,1024,104]{1,2,0:T(8,128)(2,1)} %bitcast.198), calls=%async_computation.5 | async-start | bytes 6815744 | tf_op jit(solution)/shard_map/all_to_all | solution.py:154
  420.2 103.6 %all-reduce.26.cloned.1.call-start = ((), (), s32[]{:S(2)}) async-start(), calls=%async_computation.9 | async-start | bytes 3145728 | tf_op jit(solution)/shard_map/psum | solution.py:85
  426.5 311.8 %all-reduce.22.cloned.1.call-start = ((), (), s32[]{:S(2)}) async-start(), calls=%async_computation.7 | async-start | bytes 10223616 | tf_op jit(solution)/shard_map/psum | solution.py:181
  570.4 264.4 %all-reduce.24.cloned.1.call-start = ((), (), s32[]{:S(2)}) async-start(), calls=%async_computation.8 | async-start | bytes 3145728 | tf_op jit(solution)/shard_map/psum | solution.py:85
  (42 other events, 738.9 us)
Sparse Core Ops, SparseCore 0:
  426.6 97.1 all-reduce.25
  570.5 167.7 all-reduce.21
  745.2 89.4 all-reduce.23
where the time goes:
time: 848 us; the launch traced here: 845 us
  blocking collectives  322 us (38%)
  waiting for transfers between devices  281 us (33%)
  starting transfers between devices  91.1 us (11%)
  local copies, waits for them, and re-layouts  72.4 us (9%)
  matrix products  51.2 us (6%)
  between operations  15.3 us (2%)
  other arithmetic  11.8 us (1%)
    psum x2, waiting for transfers between devices, row_total(): return lax.psum(partial_value, 'row')  185 us
    psum x2, blocking collectives, block_norm(): lax.psum(jnp.sum(widened * widened, axis=-1, keepdims=True), 'col')  91.4 us
    psum x1, waiting for transfers between devices, on_device(): gate, upper = lax.psum((gate_part, upper_part), 'col')  83.7 us
    all_to_all x1, blocking collectives, on_device(): lax.all_to_all(down_weight, 'col', split_axis=1, concat_axis=0, tiled=True)  81.9 us
    unnamed x1, blocking collectives  78.2 us
    unnamed x24, starting transfers between devices  72.7 us
    unnamed x109, local copies, waits for them, and re-layouts  44.7 us
    all_gather x2, blocking collectives, on_device(): lax.all_gather(head_count, 'col', axis=0, tiled=True)  44.2 us
  transfers between devices with their start and end apart: 31, of which 4 were waited for; matrix products, arithmetic and copies ran while one was open for 22% of the time, Pallas kernels for 0%

commit v1 on v0

v1 whole, which is shorter than its diff:
```python
import functools

import jax
import jax.numpy as jnp
from jax import lax
from jax.experimental import pallas as pl
from jax.experimental.pallas import tpu as pltpu
from jax.sharding import PartitionSpec as P

WIDTH = 16384
HEAD = 128
STEPS = 2
SLOTS = 1024
EPS = 1e-05
THETA = 500000.0
ROWS = 192
LOCAL = 12
FFL = 104
BF = jnp.bfloat16
F32 = jnp.float32
MESH = pl.DeviceIdType.MESH
ORDERS = (("x", "y", "z"), ("y", "z", "x"), ("z", "x", "y"))
NT = (((1,), (1,)), ((), ()))


def coords():
    row = lax.axis_index("row")
    col = lax.axis_index("col")
    return dict(x=(row // 4) * 2 + (col // 2) % 2, y=row % 4, z=col // 4, k=col % 2)


def device(c):
    return {"row": (c["x"] // 2) * 4 + c["y"], "col": c["z"] * 4 + (c["x"] % 2) * 2 + c["k"]}


def moved(c, d, s):
    e = dict(c)
    e[d] = (c[d] + s + 4) % 4
    return e


def remote(src, dst, ss, rs, target):
    return pltpu.make_async_remote_copy(
        src_ref=src, dst_ref=dst, send_sem=ss, recv_sem=rs, device_id=target, device_id_type=MESH
    )


def width_of(full):
    return 1024 if "x" in full else 512


def block(ref, t, c, full, d, q, half=None):
    pos = dict(c)
    pos[d] = q
    z = slice(None) if "z" in full else pos["z"]
    y = slice(None) if "y" in full else pos["y"]
    w = width_of(full)
    if "x" in full:
        xl, base = slice(None), 0
    else:
        xl, base = pos["x"] % 2, (pos["x"] // 2) * 512
    if half is not None:
        w = w // 2
        base = base + half * w
    if not isinstance(base, int):
        base = pl.multiple_of(base, 256)
    return ref.at[z, xl, y, t, :, pl.ds(base, w)]


def lead_shape(full):
    return ((4,) if "z" in full else ()) + ((2,) if "x" in full else ()) + ((4,) if "y" in full else ())


def lead_index(shape, n):
    idx = []
    for size in reversed(shape):
        idx.append(n % size)
        n = n // size
    return tuple(reversed(idx))


def for_pieces(shape, body):
    total = 1
    for size in shape:
        total *= size
    if total == 1:
        body(())
    else:

        def step(n, carry):
            body(lead_index(shape, n))
            return carry

        lax.fori_loop(0, total, step, 0)


WAYS = ((0, 1), (1, -1))


def counted(ref, n):
    return {9: ref.at[0, 0, pl.ds(0, 3), :, :, pl.ds(0, 512)], 36: ref.at[0, :, pl.ds(0, 3)]}.get(
        n, ref.at[pl.ds(0, n // 48)]
    )


def wait_sent(ref, n, sem):
    part = counted(ref, n)
    pltpu.make_async_copy(part, part, sem).wait()


def gather(g, c, ss, rs):
    def send(src, d, s, ph, sem):
        remote(src, src, ss.at[ph], rs.at[sem], device(moved(c, d, s))).start()

    for ph in range(2):
        for o in (1, 3, 2):
            for t in range(3):
                d = ORDERS[t][ph]
                send(block(g, t, c, ORDERS[t][:ph], d, c[d]), d, o, ph, ph)
        yield
        wait_sent(g, 9 * 4**ph, rs.at[ph])
    axes = [(t, ORDERS[t][2], ORDERS[t][:2]) for t in range(3)]
    for part in (0, 1):
        for t, d, full in axes:
            for i, s in WAYS:
                h = i if part == 0 else 1 - i
                send(block(g, t, c, full, d, c[d], h), d, s, 2, 3 + 2 * t + i if part == 0 else 2)
    yield
    for t, d, full in axes:
        for i, s in WAYS:
            h = block(g, t, c, full, d, (c[d] - s + 4) % 4, i)
            pltpu.make_async_copy(h, h, rs.at[3 + 2 * t + i]).wait()
            send(h, d, s, 2, 2)
    yield
    wait_sent(g, 96, rs.at[2])
    for ph in range(3):
        wait_sent(g, (9, 36, 144)[ph], ss.at[ph])


def scatter(p, fwd, land, c, ss, rs):
    def send(src, dst, d, s, st, sem):
        remote(src, dst, ss.at[st], rs.at[sem], device(moved(c, d, s))).start()

    axes = [(t, ORDERS[t][2], ORDERS[t][:2]) for t in range(3)]

    def half(t, i, full, h):
        w = width_of(full) // 2
        lead = (slice(None),) * len(lead_shape(full))
        return land[t][0].at[(i,) + lead + (slice(None), pl.ds(h * w, w))]

    for t, d, full in axes:
        for i, s in WAYS:
            send(block(p, t, c, full, d, (c[d] + 2) % 4, i), fwd[t].at[i], d, s, 0, 3 + 2 * t + i)
    for t, d, full in axes:
        for i, s in WAYS:
            send(block(p, t, c, full, d, (c[d] + s + 4) % 4, 1 - i), half(t, i, full, 1 - i), d, s, 0, 0)
    yield
    for t, d, full in axes:
        for i, s in WAYS:
            f = fwd[t].at[i]
            pltpu.make_async_copy(f, f, rs.at[3 + 2 * t + i]).wait()
            mine = block(p, t, c, full, d, (c[d] + s + 4) % 4, i)

            def add(idx, mine=mine, t=t, i=i):
                a = mine[idx].astype(F32) + fwd[t][(i,) + idx].astype(F32)
                mine[idx] = a.astype(BF)

            for_pieces(lead_shape(full), add)
            send(mine, half(t, i, full, i), d, s, 0, 0)
    yield
    wait_sent(p, 96, rs.at[0])
    for t, d, full in axes:
        mine = block(p, t, c, full, d, c[d])

        def total(idx, mine=mine, t=t):
            a = mine[idx].astype(F32) + (land[t][0][(0,) + idx].astype(F32) + land[t][0][(1,) + idx].astype(F32))
            mine[idx] = a.astype(BF)

        for_pieces(lead_shape(full), total)
    for st in (1, 2):
        axes = [(t, ORDERS[t][2 - st], ORDERS[t][: 2 - st]) for t in range(3)]
        for o in (1, 3, 2):
            for t, d, full in axes:
                send(block(p, t, c, full, d, (c[d] + o) % 4), land[t][st].at[o - 1], d, o, st, st)
        yield
        wait_sent(p, 36 // 4 ** (st - 1), rs.at[st])
        for t, d, full in axes:
            mine = block(p, t, c, full, d, c[d])

            def total(idx, mine=mine, t=t, st=st):
                a = mine[idx].astype(F32)
                for o in range(3):
                    a = a + land[t][st][(o,) + idx].astype(F32)
                mine[idx] = a.astype(BF)

            for_pieces(lead_shape(full), total)
    for st in range(3):
        wait_sent(p, (144, 36, 9)[st], ss.at[st])


def iota(shape, d):
    return lax.broadcasted_iota(jnp.int32, shape, d)


def onehot(cond):
    return jnp.where(cond, 1.0, 0.0).astype(BF)


def mm(a, b):
    return jnp.dot(a, b, preferred_element_type=F32)


def mm_nt(a, b):
    return lax.dot_general(a, b, NT, preferred_element_type=F32)


def kernel(*refs):
    names = (
        "emb_h", "attn_gain", "ffn_gain", "wq_h", "kh_h", "vh_h", "wo_h", "g_h", "u_h", "wd_h", "kc_h", "vc_h", "lens",
        "pos", "freq", "out", "app", "g", "p", "emb", "wq", "kv", "wo", "gate", "up", "wd", "kc", "vc", "ginv",
        "acc", "ssq", "qs", "qr", "kn", "vn", "qb", "sbuf", "pb", "ho", "hr", "xs", "xr", "res", "fin", "to_rows",
        "to_tokens", "by_row", "by_head", "spread", "place", "load_sem", "load_out", "pair_s", "pair_r", "ag_s",
        "ag_r", "rs_s", "rs_r", "a2a_s", "a2a_r", "gi_s", "gi_r", "x_s", "x_r", "f_s", "f_r",
    )
    n = dict(zip(names, refs[: len(names)]))
    rest = refs[len(names) :]
    r = type("Refs", (), n)
    c = coords()
    k = c["k"]
    col = lax.axis_index("col")
    row = lax.axis_index("row")
    xl, xh, y, z = c["x"] % 2, c["x"] // 2, c["y"], c["z"]
    mate = {"row": row, "col": col + 1 - 2 * k}
    far = dict(c)
    far["x"] = (c["x"] + 2) % 4

    def peer(o):
        return {"row": row, "col": (col + o) % 16}

    loads = {}

    def load(name, i, src, dst):
        cp = pltpu.make_async_copy(src, dst, r.load_sem.at[i])
        cp.start()
        loads[name] = cp

    load("emb", 0, r.emb_h, r.emb)

    bar = pltpu.get_barrier_semaphore()
    greet = [peer(o) for o in range(1, 16)]
    greet += [device(moved(c, "y", 1)), device(moved(c, "y", 2)), device(moved(c, "y", 3)), device(far)]
    other = dict(c)
    other["x"] = (c["x"] + 3 - 2 * (c["x"] % 2)) % 4
    greet.append(device(other))
    for target in greet:
        pl.semaphore_signal(bar, inc=1, device_id=target, device_id_type=MESH)
    pl.semaphore_wait(bar, len(greet))

    pair = {}

    def share(i, src_of, dst, blocks):
        for b in blocks:
            remote(src_of(1 - k, b), dst.at[(k,) + b], r.pair_s.at[i], r.pair_r.at[i], mate).start()
            pltpu.make_async_copy(src_of(k, b), dst.at[(k,) + b], r.load_sem.at[i]).start()

    def share_wait(i, dst):
        pltpu.make_async_copy(dst.at[k], dst.at[k], r.load_sem.at[i]).wait()
        whole = remote(dst.at[k], dst.at[1 - k], r.pair_s.at[i], r.pair_r.at[i], mate)
        whole.wait_recv()
        pair[i] = whole

    def lanes(ref):
        return lambda par, b: ref.at[:, pl.ds(pl.multiple_of((2 * b[0] + par) * 1024, 1024), 1024)]

    eight = [(b,) for b in range(8)]

    ga = r.attn_gain[...].astype(F32).reshape(1, 1024)
    gf = r.ffn_gain[...].astype(F32).reshape(1, 1024)
    r.ginv[z * 2 + xl] = jnp.where(iota((8, 1024), 0) == 0, 1.0 / (ga * ga), 1.0 / (gf * gf))

    def own(ref, t):
        return block(ref, t, c, (), "z", z)

    loads["emb"].wait()
    gain_a = jnp.where(xh == 0, ga[:, :512], ga[:, 512:])
    gain_f = jnp.where(xh == 0, gf[:, :512], gf[:, 512:])

    def emb_piece(s, t):
        return r.emb[s, y, t, :, pl.ds(pl.multiple_of(xh * 512, 512), 512)].astype(F32)

    def startup():
        for o in range(1, 8):
            dst = r.ginv.at[z * 2 + xl]
            remote(dst, dst, r.gi_s.at[0], r.gi_r.at[0], peer(2 * o)).start()
        share(1, lambda par, b: r.wq_h.at[:, par], r.wq, [()])
        share(2, lanes(r.kh_h), r.kv.at[0], eight)
        share(9, lanes(r.vh_h), r.kv.at[1], eight)
        load("kc", 7, r.kc_h, r.kc)
        load("vc", 8, r.vc_h, r.vc)
        share(3, lanes(r.wo_h), r.wo, eight)
        share(4, lanes(r.g_h), r.gate, eight)
        share(5, lanes(r.u_h), r.up, eight)
        share(6, lanes(r.wd_h), r.wd, eight)
        a, b = iota((256, ROWS), 0), iota((256, ROWS), 1)
        r.to_rows[...] = onehot(((a & 15) < LOCAL) & (b == (a >> 4) * LOCAL + (a & 15)))
        a, b = iota((ROWS, 256), 0), iota((ROWS, 256), 1)
        r.to_tokens[...] = onehot(((b & 15) < LOCAL) & (a == (b >> 4) * LOCAL + (b & 15)))
        r.by_row[...] = onehot(((a >> 4) == (b & 15)) & ((a & 15) == (b >> 4)))
        a, b = iota((256, ROWS), 0), iota((256, ROWS), 1)
        r.by_head[...] = onehot(((b >> 4) == (a & 15)) & ((b & 15) == (a >> 4)))
        a, b = iota((ROWS, 16), 0), iota((ROWS, 16), 1)
        r.spread[...] = onehot((a >> 4) == b)
        a, b = iota((128, 256), 0), iota((128, 256), 1)
        for src in range(16):
            head_col = (a >> 4) * 8 + (a & 7) + (src // 2) * 16 + ((a >> 3) & 1) * 128
            r.place[src] = onehot((a < 32) & (b == head_col))

    first = {"w": True}

    def squares(s, g, zz, xx, which):
        v = g[zz, xx].reshape(ROWS, 1024)
        gi_row = r.ginv[zz * 2 + xx, pl.ds(which, 1), :]
        acc = jnp.zeros((ROWS, 128), F32)
        for j in range(8):
            w = v[:, j * 128 : (j + 1) * 128].astype(F32)
            acc = acc + w * w * gi_row[:, j * 128 : (j + 1) * 128]
        r.ssq[s] += acc

    def stream(s):
        sends = []
        g, p = r.g.at[s], r.p.at[s]
        fwd = [rest[t * 4].at[s] for t in range(3)]
        land = [[rest[t * 4 + 1 + st].at[s] for st in range(3)] for t in range(3)]
        for t in range(3):
            own(g, t)[...] = (emb_piece(s, t) * gain_a).astype(BF)
        it = gather(g, c, r.ag_s.at[s], r.ag_r.at[s])
        next(it)
        if s == 0:
            startup()
        yield
        yield from it

        if first.pop("w", False):
            share_wait(1, r.wq)
            share_wait(2, r.kv.at[0])
            share_wait(9, r.kv.at[1])
            part = r.ginv.at[pl.ds(0, 7)]
            pltpu.make_async_copy(part, part, r.gi_r.at[0]).wait()
        r.acc[s] = jnp.zeros((3, ROWS, 128), F32)
        r.ssq[s] = jnp.zeros((ROWS, 128), F32)

        def qkv(i, carry):
            zz, xx = i // 2, i % 2
            v = g[zz, xx].reshape(ROWS, 1024)
            wq = jnp.concatenate([r.wq[0, i], r.wq[1, i]], axis=1)
            q = mm(v, wq)
            r.acc[s, 0] += q[:, :128]
            r.acc[s, 1] += q[:, 128:]
            wkv = [r.kv[j, core, i].astype(F32) for core in range(2) for j in range(2)]
            wkv = jnp.concatenate(wkv, axis=0).astype(BF)
            r.acc[s, 2, :, pl.ds(0, 32)] += mm_nt(v, wkv)
            squares(s, g, zz, xx, 0)
            return carry

        lax.fori_loop(0, 4, qkv, 0)
        yield
        lax.fori_loop(4, 8, qkv, 0)
        total = jnp.sum(r.ssq[s], axis=-1, keepdims=True)
        high = total.astype(BF).astype(F32)
        low = total - high
        lane = iota((ROWS, 128), 1)
        tail = jnp.where(lane == 32, high, jnp.where(lane == 33, low, r.acc[s, 2]))
        sums = jnp.concatenate([r.acc[s, 0], r.acc[s, 1], tail], axis=1).astype(BF)
        r.qs[s] = mm(r.to_rows[...], sums).astype(BF).reshape(16, 16, 384)
        for o in range(1, 16):
            remote(r.qs.at[s, (col + o) % 16], r.qr.at[s, col], r.a2a_s.at[s, 0], r.a2a_r.at[s, 0], peer(o)).start()
        r.qr[s, col] = r.qs[s, col]
        yield
        part = r.qr.at[s, pl.ds(0, 15)]
        pltpu.make_async_copy(part, part, r.a2a_r.at[s, 0]).wait()

        ends = r.qr[s, 0, :, pl.ds(256, 128)].astype(F32) + r.qr[s, 1, :, pl.ds(256, 128)].astype(F32)
        l16 = iota((16, 128), 1)
        square = jnp.sum(jnp.where((l16 == 32) | (l16 == 33), ends, 0.0), axis=-1, keepdims=True)
        scale = lax.rsqrt(square / WIDTH + EPS)
        angle = jnp.zeros((16, 128), jnp.int32)
        for j in range(LOCAL):
            angle = jnp.where(iota((16, 128), 0) == j, r.pos[j] + s, angle)
        angle = angle.astype(F32) * r.freq[...]
        cos, sin = jnp.cos(angle), jnp.sin(angle)
        sin = jnp.where(l16 < 64, -sin, sin)

        def rotate(v):
            return (v * cos + pltpu.roll(v, 64, 1) * sin).astype(BF)

        heads = []
        for h in range(8):
            both = r.qr[s, 2 * h, :, pl.ds(0, 256)].astype(F32) + r.qr[s, 2 * h + 1, :, pl.ds(0, 256)].astype(F32)
            both = both * scale
            heads += [rotate(both[:, :128]), rotate(both[:, 128:])]
        q_all = mm(r.by_row[...], jnp.concatenate(heads, axis=0)).astype(BF)
        r.qb[s] = q_all
        kv = mm(r.qr[s, 0, :, pl.ds(256, 128)], r.place[0])
        for src in range(1, 16):
            kv = kv + mm(r.qr[s, src, :, pl.ds(256, 128)], r.place[src])
        kv = kv * scale
        r.kn[s] = rotate(kv[:, :128])
        r.vn[s] = kv[:, 128:].astype(BF)
        r.app[s, 0] = r.kn[s]
        r.app[s, 1] = r.vn[s]

        if s == 0:
            loads["kc"].wait()
            loads["vc"].wait()
        factor = 1.0 / (HEAD**0.5)
        slot = iota((16, SLOTS), 1)
        qf = r.qb[s].astype(F32)
        fresh = []
        top = None
        for s2 in range(s + 1):
            sc = jnp.sum(qf * mm(r.spread[...], r.kn[s2]), axis=-1, keepdims=True) * factor
            fresh.append(sc)
            top = sc if top is None else jnp.maximum(top, sc)
        for j in range(LOCAL):
            sc = mm_nt(r.qb[s, pl.ds(j * 16, 16), :], r.kc[j]) * factor
            r.sbuf[pl.ds(j * 16, 16), :] = jnp.where(slot < r.lens[j], sc, -1e30)
        dens = []
        tops = []
        for j in range(LOCAL):
            sc = r.sbuf[pl.ds(j * 16, 16), :]
            m = jnp.maximum(jnp.max(sc, axis=-1, keepdims=True), top[j * 16 : j * 16 + 16])
            w = jnp.exp(sc - m)
            r.pb[pl.ds(j * 16, 16), :] = w.astype(BF)
            dens.append(jnp.sum(w, axis=-1, keepdims=True))
            tops.append(m)
        den = jnp.concatenate(dens, axis=0)
        m = jnp.concatenate(tops, axis=0)
        o = jnp.concatenate([mm(r.pb[pl.ds(j * 16, 16), :], r.vc[j]) for j in range(LOCAL)], axis=0)
        for s2 in range(s + 1):
            w = jnp.exp(fresh[s2] - m)
            den = den + w
            o = o + w.astype(BF).astype(F32) * mm(r.spread[...], r.vn[s2])
        o = (o / den).astype(BF)
        ho = mm(r.by_head[...], o).astype(BF).reshape(8, 2, 16, 128)
        for h in range(8):
            r.ho[s, h] = jnp.concatenate([ho[h, 0], ho[h, 1]], axis=1)
        for o_ in range(1, 16):
            remote(
                r.ho.at[s, ((col + o_) % 16) // 2], r.hr.at[s, col], r.a2a_s.at[s, 1], r.a2a_r.at[s, 1], peer(o_)
            ).start()
        r.hr[s, col] = r.ho[s, col // 2]
        yield
        if s == 0:
            share_wait(3, r.wo)
        part = r.hr.at[s, pl.ds(0, 15)]
        pltpu.make_async_copy(part, part, r.a2a_r.at[s, 1]).wait()

        attn = mm(r.to_tokens[...], r.hr[s].reshape(256, 256)).astype(BF)

        def project(i, carry):
            w = jnp.concatenate([r.wo[0, i], r.wo[1, i]], axis=0)
            p[i // 2, i % 2] = mm(attn, w).astype(BF).reshape(4, 3, 16, 1024)
            return carry

        lax.fori_loop(0, 8, project, 0)
        yield from scatter(p, fwd, land, c, r.rs_s.at[s], r.rs_r.at[s])
        for t in range(3):
            v = (emb_piece(s, t) + own(p, t)[...].astype(F32)).astype(BF)
            r.res[s, t] = v
            own(g, t)[...] = (v.astype(F32) * gain_f).astype(BF)
        yield from gather(g, c, r.ag_s.at[s], r.ag_r.at[s])

        if s == 0:
            share_wait(4, r.gate)
            share_wait(5, r.up)
        gap = jnp.zeros((128 - FFL, 1024), BF)
        r.xs[s] = jnp.zeros((4, ROWS, 128), F32)
        r.ssq[s] = jnp.zeros((ROWS, 128), F32)

        def slab(i, carry):
            zz, xx = i // 2, i % 2
            v = g[zz, xx].reshape(ROWS, 1024)
            for core in range(2):
                w = jnp.concatenate([r.gate[core, i], gap, r.up[core, i], gap], axis=0)
                v2 = mm_nt(v, w)
                r.xs[s, core] += v2[:, :128]
                r.xs[s, 2 + core] += v2[:, 128:]
            squares(s, g, zz, xx, 1)
            return carry

        lax.fori_loop(0, 4, slab, 0)
        yield
        lax.fori_loop(4, 8, slab, 0)
        total = jnp.sum(r.ssq[s], axis=-1, keepdims=True)
        r.xs[s, 0] = jnp.where(lane < FFL, r.xs[s, 0], total)
        cp = remote(r.xs.at[s], r.xr.at[s], r.x_s.at[s], r.x_r.at[s], mate)
        cp.start()
        yield
        if s == 0:
            share_wait(6, r.wd)
        cp.wait()
        first_sum = r.xs[s, 0] + r.xr[s, 0]
        square = jnp.sum(jnp.where(lane == FFL, first_sum, 0.0), axis=-1, keepdims=True)
        scale = lax.rsqrt(square / WIDTH + EPS)
        hidden = []
        for core in range(2):
            gate = (first_sum if core == 0 else r.xs[s, core] + r.xr[s, core]) * scale
            up = (r.xs[s, 2 + core] + r.xr[s, 2 + core]) * scale
            act = gate / (1.0 + jnp.exp(-gate)) * up
            hidden.append(jnp.where(lane < FFL, act, 0.0).astype(BF))
        hidden = jnp.concatenate(hidden, axis=1)

        def down(i, carry):
            v = mm(hidden, jnp.concatenate([r.wd[0, i], gap, r.wd[1, i], gap], axis=0))
            p[i // 2, i % 2] = v.astype(BF).reshape(4, 3, 16, 1024)
            return carry

        lax.fori_loop(0, 8, down, 0)
        yield from scatter(p, fwd, land, c, r.rs_s.at[s], r.rs_r.at[s])

        def fpiece(yy, hh):
            return r.fin.at[s, yy, :, :, pl.ds(pl.multiple_of(hh * 512, 512), 512)]

        for t in range(3):
            v = r.res[s, t].astype(F32) + own(p, t)[...].astype(F32)
            r.fin[s, y, t, :, pl.ds(pl.multiple_of(xh * 512, 512), 512)] = v.astype(BF)
        mine = fpiece(y, xh)

        def fsend(piece, target, i):
            cp = remote(piece, piece, r.f_s.at[s, i], r.f_r.at[s, i], target)
            cp.start()
            sends.append(cp)

        def farrive(piece, i):
            remote(piece, piece, r.f_s.at[s, i], r.f_r.at[s, i], mate).wait_recv()

        fsend(mine, device(far), 0)
        for o_ in (1, 3, 2):
            fsend(mine, device(moved(c, "y", o_)), o_)
        yield
        theirs = fpiece(y, 1 - xh)
        farrive(theirs, 0)
        for o_ in (1, 3, 2):
            fsend(theirs, device(moved(c, "y", o_)), 3 + o_)
        yield
        for o_ in (1, 2, 3):
            farrive(fpiece((y + 4 - o_) % 4, xh), o_)
        for o_ in (1, 2, 3):
            farrive(fpiece((y + 4 - o_) % 4, 1 - xh), 3 + o_)
        cp = pltpu.make_async_copy(r.fin.at[s], r.out.at[s], r.load_out.at[s])
        cp.start()
        for e in sends:
            e.wait_send()
        for i, ref in ((0, r.qr), (1, r.hr)):
            part = ref.at[s, pl.ds(0, 15)]
            pltpu.make_async_copy(part, part, r.a2a_s.at[s, i]).wait()
        cp.wait()

    live = [stream(s) for s in range(STEPS)]
    for s in SCHEDULE:
        next(live[int(s)], None)
    for it in live:
        for _ in it:
            pass
    part = r.ginv.at[pl.ds(0, 7)]
    pltpu.make_async_copy(part, part, r.gi_s.at[0]).wait()
    for i in pair:
        pair[i].wait_send()


SCHEDULE = "0101001" + "01" * 22


def rope_frequency(head_size):
    half_size = head_size // 2
    return THETA ** (-2.0 * jnp.arange(half_size, dtype=jnp.float32) / head_size)


def on_device(
    embeds,
    attn_gain,
    ffn_gain,
    query_weight,
    key_matrix,
    value_matrix,
    output_weight,
    gate_weight,
    up_weight,
    down_weight,
    rotated_key_cache,
    stored_value_cache,
    lengths,
    positions,
):
    freq = rope_frequency(HEAD)
    freq = jnp.concatenate([freq, freq]).reshape(1, HEAD)
    anyspace = pl.BlockSpec(memory_space=pl.ANY)
    vmem = pl.BlockSpec(memory_space=pltpu.VMEM)
    smem = pl.BlockSpec(memory_space=pltpu.SMEM)
    scratch = [
        pltpu.VMEM((2, 4, 2, 4, 3, 16, 1024), BF),
        pltpu.VMEM((2, 4, 2, 4, 3, 16, 1024), BF),
        pltpu.VMEM((2, 4, 3, 16, 1024), BF),
        pltpu.VMEM((2, 8, 1024, 128), BF),
        pltpu.VMEM((2, 2, 8, 8, 1024), BF),
        pltpu.VMEM((2, 8, 128, 1024), BF),
        pltpu.VMEM((2, 8, FFL, 1024), BF),
        pltpu.VMEM((2, 8, FFL, 1024), BF),
        pltpu.VMEM((2, 8, FFL, 1024), BF),
        pltpu.VMEM((LOCAL, SLOTS, HEAD), BF),
        pltpu.VMEM((LOCAL, SLOTS, HEAD), BF),
        pltpu.VMEM((8, 8, 1024), F32),
        pltpu.VMEM((2, 3, ROWS, 128), F32),
        pltpu.VMEM((2, ROWS, 128), F32),
        pltpu.VMEM((2, 16, 16, 384), BF),
        pltpu.VMEM((2, 16, 16, 384), BF),
        pltpu.VMEM((2, 16, 128), BF),
        pltpu.VMEM((2, 16, 128), BF),
        pltpu.VMEM((2, ROWS, 128), BF),
        pltpu.VMEM((ROWS, SLOTS), F32),
        pltpu.VMEM((ROWS, SLOTS), BF),
        pltpu.VMEM((2, 8, 16, 256), BF),
        pltpu.VMEM((2, 16, 16, 256), BF),
        pltpu.VMEM((2, 4, ROWS, 128), F32),
        pltpu.VMEM((2, 4, ROWS, 128), F32),
        pltpu.VMEM((2, 3, 16, 512), BF),
        pltpu.VMEM((2, 4, 3, 16, 1024), BF),
        pltpu.VMEM((256, ROWS), BF),
        pltpu.VMEM((ROWS, 256), BF),
        pltpu.VMEM((ROWS, 256), BF),
        pltpu.VMEM((256, ROWS), BF),
        pltpu.VMEM((ROWS, 16), BF),
        pltpu.VMEM((16, 128, 256), BF),
        pltpu.SemaphoreType.DMA((10,)),
        pltpu.SemaphoreType.DMA((2,)),
        pltpu.SemaphoreType.DMA((10,)),
        pltpu.SemaphoreType.DMA((10,)),
        pltpu.SemaphoreType.DMA((2, 3)),
        pltpu.SemaphoreType.DMA((2, 9)),
        pltpu.SemaphoreType.DMA((2, 3)),
        pltpu.SemaphoreType.DMA((2, 9)),
        pltpu.SemaphoreType.DMA((2, 2)),
        pltpu.SemaphoreType.DMA((2, 2)),
        pltpu.SemaphoreType.DMA((1,)),
        pltpu.SemaphoreType.DMA((1,)),
        pltpu.SemaphoreType.DMA((2,)),
        pltpu.SemaphoreType.DMA((2,)),
        pltpu.SemaphoreType.DMA((2, 7)),
        pltpu.SemaphoreType.DMA((2, 7)),
    ]
    for t in range(3):
        full = ORDERS[t][:2]
        scratch.append(pltpu.VMEM((2, 2) + lead_shape(full) + (16, width_of(full) // 2), BF))
        for st in range(3):
            full = ORDERS[t][: 2 - st]
            scratch.append(pltpu.VMEM((2, 3 if st else 2) + lead_shape(full) + (16, width_of(full)), BF))
    out, app = pl.pallas_call(
        kernel,
        out_shape=(
            jax.ShapeDtypeStruct((2, 4, 3, 16, 1024), BF),
            jax.ShapeDtypeStruct((2, 2, 16, 128), BF),
        ),
        in_specs=[anyspace, vmem, vmem] + [anyspace] * 9 + [smem, smem, vmem],
        out_specs=(anyspace, vmem),
        scratch_shapes=scratch,
        compiler_params=pltpu.CompilerParams(
            collective_id=0, has_side_effects=True, vmem_limit_bytes=63 * 1024 * 1024
        ),
    )(
        embeds.reshape(2, 4, 3, 16, 1024),
        attn_gain,
        ffn_gain,
        query_weight.reshape(8, 2, 1024, 128),
        key_matrix.T,
        value_matrix.T,
        output_weight,
        gate_weight.T,
        up_weight.T,
        down_weight,
        rotated_key_cache.reshape(LOCAL, SLOTS, HEAD),
        stored_value_cache.reshape(LOCAL, SLOTS, HEAD),
        lengths,
        positions,
        freq,
    )
    return out.reshape(2, ROWS, 1024), app[:, :, :LOCAL].transpose(0, 2, 1, 3)


def solution(mesh):
    in_specs = (
        P(None, None, "col"),
        P("col"),
        P("col"),
        P(None, ("row", "col")),
        P(None, ("row", "col")),
        P(None, ("row", "col")),
        P(("row", "col"), None),
        P(None, ("row", "col")),
        P(None, ("row", "col")),
        P(("row", "col"), None),
        P("col", "row", None, None),
        P("col", "row", None, None),
        P("col"),
        P("col"),
    )
    out_specs = (P(None, None, "col"), P(None, "col", None, "row"))
    return jax.shard_map(on_device, mesh=mesh, in_specs=in_specs, out_specs=out_specs, check_vma=False)
```

time: 848 us -> 162 us (0.19)
  blocking collectives: 322 us -> 0 us
  waiting for transfers between devices: 281 us -> 0 us
  Pallas kernels: 0 us -> 157 us
  starting transfers between devices: 91.1 us -> 0 us
  local copies, waits for them, and re-layouts: 72.4 us -> 3.39 us
  matrix products: 51.2 us -> 0 us
  between operations: 15.3 us -> 0.64 us
  other arithmetic: 11.8 us -> 0.6 us
    psum x3 -> x0, waiting for transfers between devices: 269 us -> none  [the longest x2 185 us: row_total(): return lax.psum(partial_value, 'row')]
    pallas_call x0 -> x1, Pallas kernels: none -> 157 us  [on_device(): pl.pallas_call(kernel, out_shape=(jax.ShapeDtypeStruct((2, 4, 3, 16, 1024...]
    all_to_all x3 -> x0, blocking collectives: 108 us -> none  [the longest x1 81.9 us: on_device(): lax.all_to_all(down_weight, 'col', split_axis=1, concat_axis=0, tiled=True)]
    psum x2 -> x0, blocking collectives: 91.4 us -> none  [block_norm(): lax.psum(jnp.sum(widened * widened, axis=-1, keepdims=True), 'col')]
    unnamed x1 -> x0, blocking collectives: 78.2 us -> none
    unnamed x24 -> x0, starting transfers between devices: 72.7 us -> none
    dot_general x21 -> x0, matrix products: 51.2 us -> none  [the longest x2 8.78 us: on_device(): jnp.dot(normed_ffn, gate_block, preferred_element_type=jnp.float32)]
    all_gather x2 -> x0, blocking collectives: 44.2 us -> none  [on_device(): lax.all_gather(head_count, 'col', axis=0, tiled=True)]
  transfers between devices with their start and end apart: 31 -> 0, of which waited for: 4 -> 0; matrix products, arithmetic and copies ran while one was open for 22% -> 0% of each run, Pallas kernels for 0% -> 0%
where the time goes in v1:
time: 162 us
  Pallas kernels  157 us (97%)
  local copies, waits for them, and re-layouts  3.39 us (2%)
    pallas_call x1, Pallas kernels, on_device(): pl.pallas_call(kernel, out_shape=(jax.ShapeDtypeStruct((2, 4, 3, 16, 1024...  157 us

profile of v1, /device:TPU:0, one launch (start us, length us, event | category | flops | bytes accessed | tf_op | source)
XLA Modules:
  0.0 161.8 jit_solution(3415336717743383965)
XLA Ops:
  0.6 0.6 maximum_bitcast_fusion.refs_14_
  1.2 157.1 %shard_map.149 = (bf16[2,4,3,16,1024]{4,3,2,1,0:T(8,128)(2,1)}, bf16[2,2,16,128]{3,2,1,0:T(8,128)(2,1)}) custom-call(bf16[2,4,3,16,1024]{4,3,2,1,0:T(8,128)(2,1)} %bitcast.18, bf16[1024]{0:T(1024)(128)(2,1)} %refs_1_.1, bf16[1024]{0:T(1024)(128)(2,1)} %refs_2_.1, bf16[8,2,1024,128]{3,2,1,0:T(8,128)(2,1)} %bitcast.13, bf16[8,16384]{1,0:T(8,128)(2,1)} %bitcast.20, ...), custom_call_target="tpu_custom_call" | custom-call | tf_op jit(solution)/shard_map/pallas_call | solution.py:657
  158.4 0.7 slice_bitcast_fusion
  159.1 0.6 copy.16
  159.7 2.1 %copy.18 = bf16[2,192,1024]{2,1,0:T(8,128)(2,1)} copy(bf16[2,192,1024]{2,1,0:T(8,128)(2,1)} %bitcast.19) | data formatting | bytes 1572864
  (1 shorter events, 0.0 us)

commit v2 on v1

--- a/solution.py
+++ b/solution.py
@@ -21,6 +21,7 @@
 MESH = pl.DeviceIdType.MESH
 ORDERS = (("x", "y", "z"), ("y", "z", "x"), ("z", "x", "y"))
 NT = (((1,), (1,)), ((), ()))
+FAR_FIRST = (8, 9, 7, 10, 6, 11, 5, 12, 4, 13, 3, 14, 2, 15, 1)
 
 
 def coords():
@@ -45,70 +46,60 @@
     )
 
 
-def width_of(full):
-    return 1024 if "x" in full else 512
-
-
-def block(ref, t, c, full, d, q, half=None):
+def block(ref, t, c, full, d, q, sub, half=None):
     pos = dict(c)
     pos[d] = q
     z = slice(None) if "z" in full else pos["z"]
     y = slice(None) if "y" in full else pos["y"]
-    w = width_of(full)
-    if "x" in full:
-        xl, base = slice(None), 0
-    else:
-        xl, base = pos["x"] % 2, (pos["x"] // 2) * 512
-    if half is not None:
-        w = w // 2
-        base = base + half * w
-    if not isinstance(base, int):
-        base = pl.multiple_of(base, 256)
-    return ref.at[z, xl, y, t, :, pl.ds(base, w)]
+    xl = slice(None) if "x" in full else pos["x"] % 2
+    xh = slice(None) if "x" in full else pos["x"] // 2
+    columns = pl.ds(sub * 256, 256) if half is None else pl.ds(sub * 256 + half * 128, 128)
+    return ref.at[z, xl, xh, y, t, :, columns]
 
 
 def lead_shape(full):
-    return ((4,) if "z" in full else ()) + ((2,) if "x" in full else ()) + ((4,) if "y" in full else ())
-
-
-def lead_index(shape, n):
-    idx = []
-    for size in reversed(shape):
-        idx.append(n % size)
-        n = n // size
-    return tuple(reversed(idx))
-
-
-def for_pieces(shape, body):
-    total = 1
-    for size in shape:
-        total *= size
-    if total == 1:
+    return ((4,) if "z" in full else ()) + ((2, 2) if "x" in full else ()) + ((4,) if "y" in full else ())
+
+
+def for_parts(shape, body):
+    if len(shape) < 2:
         body(())
     else:
 
         def step(n, carry):
-            body(lead_index(shape, n))
+            body((n,))
             return carry
 
-        lax.fori_loop(0, total, step, 0)
+        lax.fori_loop(0, shape[0], step, 0)
 
 
 WAYS = ((0, 1), (1, -1))
 
 
 def counted(ref, n):
-    return {9: ref.at[0, 0, pl.ds(0, 3), :, :, pl.ds(0, 512)], 36: ref.at[0, :, pl.ds(0, 3)]}.get(
-        n, ref.at[pl.ds(0, n // 48)]
-    )
-
-
-def wait_sent(ref, n, sem):
+    columns = pl.ds(0, 256)
+    if n == 9:
+        return ref.at[0, 0, 0, pl.ds(0, 3), :, :, columns]
+    if n == 36:
+        return ref.at[0, :, :, pl.ds(0, 3), :, :, columns]
+    return ref.at[pl.ds(0, n // 48), :, :, :, :, :, columns]
+
+
+def wait_for(ref, n, sem):
     part = counted(ref, n)
     pltpu.make_async_copy(part, part, sem).wait()
 
 
-def gather(g, c, ss, rs):
+def drain(ref, ss, counts):
+    for i, n in enumerate(counts):
+        wait_for(ref, n, ss.at[i])
+
+
+GATHERED = (9, 36, 144)
+SCATTERED = (144, 36, 9)
+
+
+def gather(g, c, ss, rs, sub):
     def send(src, d, s, ph, sem):
         remote(src, src, ss.at[ph], rs.at[sem], device(moved(c, d, s))).start()
 
@@ -116,86 +107,86 @@
         for o in (1, 3, 2):
             for t in range(3):
                 d = ORDERS[t][ph]
-                send(block(g, t, c, ORDERS[t][:ph], d, c[d]), d, o, ph, ph)
-        yield
-        wait_sent(g, 9 * 4**ph, rs.at[ph])
+                send(block(g, t, c, ORDERS[t][:ph], d, c[d], sub), d, o, ph, ph)
+        yield
+        wait_for(g, 9 * 4**ph, rs.at[ph])
     axes = [(t, ORDERS[t][2], ORDERS[t][:2]) for t in range(3)]
     for part in (0, 1):
         for t, d, full in axes:
             for i, s in WAYS:
                 h = i if part == 0 else 1 - i
-                send(block(g, t, c, full, d, c[d], h), d, s, 2, 3 + 2 * t + i if part == 0 else 2)
+                send(block(g, t, c, full, d, c[d], sub, h), d, s, 2, 3 + 2 * t + i if part == 0 else 2)
     yield
     for t, d, full in axes:
         for i, s in WAYS:
-            h = block(g, t, c, full, d, (c[d] - s + 4) % 4, i)
+            h = block(g, t, c, full, d, (c[d] - s + 4) % 4, sub, i)
             pltpu.make_async_copy(h, h, rs.at[3 + 2 * t + i]).wait()
             send(h, d, s, 2, 2)
     yield
-    wait_sent(g, 96, rs.at[2])
-    for ph in range(3):
-        wait_sent(g, (9, 36, 144)[ph], ss.at[ph])
-
-
-def scatter(p, fwd, land, c, ss, rs):
+    wait_for(g, 96, rs.at[2])
+
+
+def scatter(p, fwd, land, c, ss, rs, sub):
     def send(src, dst, d, s, st, sem):
         remote(src, dst, ss.at[st], rs.at[sem], device(moved(c, d, s))).start()
 
     axes = [(t, ORDERS[t][2], ORDERS[t][:2]) for t in range(3)]
 
     def half(t, i, full, h):
-        w = width_of(full) // 2
         lead = (slice(None),) * len(lead_shape(full))
-        return land[t][0].at[(i,) + lead + (slice(None), pl.ds(h * w, w))]
+        return land[t][0].at[(i,) + lead + (slice(None), pl.ds(h * 128, 128))]
 
     for t, d, full in axes:
         for i, s in WAYS:
-            send(block(p, t, c, full, d, (c[d] + 2) % 4, i), fwd[t].at[i], d, s, 0, 3 + 2 * t + i)
+            send(block(p, t, c, full, d, (c[d] + 2) % 4, sub, i), fwd[t].at[i], d, s, 0, 3 + 2 * t + i)
     for t, d, full in axes:
         for i, s in WAYS:
-            send(block(p, t, c, full, d, (c[d] + s + 4) % 4, 1 - i), half(t, i, full, 1 - i), d, s, 0, 0)
+            send(block(p, t, c, full, d, (c[d] + s + 4) % 4, sub, 1 - i), half(t, i, full, 1 - i), d, s, 0, 0)
     yield
     for t, d, full in axes:
         for i, s in WAYS:
             f = fwd[t].at[i]
             pltpu.make_async_copy(f, f, rs.at[3 + 2 * t + i]).wait()
-            mine = block(p, t, c, full, d, (c[d] + s + 4) % 4, i)
+            mine = block(p, t, c, full, d, (c[d] + s + 4) % 4, sub, i)
 
             def add(idx, mine=mine, t=t, i=i):
                 a = mine[idx].astype(F32) + fwd[t][(i,) + idx].astype(F32)
                 mine[idx] = a.astype(BF)
 
-            for_pieces(lead_shape(full), add)
+            for_parts(lead_shape(full), add)
             send(mine, half(t, i, full, i), d, s, 0, 0)
     yield
-    wait_sent(p, 96, rs.at[0])
+    wait_for(p, 96, rs.at[0])
     for t, d, full in axes:
-        mine = block(p, t, c, full, d, c[d])
+        mine = block(p, t, c, full, d, c[d], sub)
 
         def total(idx, mine=mine, t=t):
             a = mine[idx].astype(F32) + (land[t][0][(0,) + idx].astype(F32) + land[t][0][(1,) + idx].astype(F32))
             mine[idx] = a.astype(BF)
 
-        for_pieces(lead_shape(full), total)
+        for_parts(lead_shape(full), total)
     for st in (1, 2):
         axes = [(t, ORDERS[t][2 - st], ORDERS[t][: 2 - st]) for t in range(3)]
         for o in (1, 3, 2):
             for t, d, full in axes:
-                send(block(p, t, c, full, d, (c[d] + o) % 4), land[t][st].at[o - 1], d, o, st, st)
-        yield
-        wait_sent(p, 36 // 4 ** (st - 1), rs.at[st])
+                send(block(p, t, c, full, d, (c[d] + o) % 4, sub), land[t][st].at[o - 1], d, o, st, st)
+        yield
+        wait_for(p, 36 // 4 ** (st - 1), rs.at[st])
         for t, d, full in axes:
-            mine = block(p, t, c, full, d, c[d])
-
-            def total(idx, mine=mine, t=t, st=st):
-                a = mine[idx].astype(F32)
-                for o in range(3):
-                    a = a + land[t][st][(o,) + idx].astype(F32)
-                mine[idx] = a.astype(BF)
-
-            for_pieces(lead_shape(full), total)
-    for st in range(3):
-        wait_sent(p, (144, 36, 9)[st], ss.at[st])
+            mine = block(p, t, c, full, d, c[d], sub)
+            a = mine[...].astype(F32)
+            for o in range(3):
+                a = a + land[t][st][o].astype(F32)
+            mine[...] = a.astype(BF)
+
+
+def in_turn(a, b):
+    for _ in a:
+        yield
+        next(b)
+        yield
+    for _ in b:
+        yield
 
 
 def iota(shape, d):
@@ -278,15 +269,25 @@
     gf = r.ffn_gain[...].astype(F32).reshape(1, 1024)
     r.ginv[z * 2 + xl] = jnp.where(iota((8, 1024), 0) == 0, 1.0 / (ga * ga), 1.0 / (gf * gf))
 
-    def own(ref, t):
-        return block(ref, t, c, (), "z", z)
+    def own(ref, t, sub):
+        return block(ref, t, c, (), "z", z, sub)
+
+    def cols(sub):
+        return pl.ds(pl.multiple_of(xh * 512 + sub * 256, 256), 256)
 
     loads["emb"].wait()
     gain_a = jnp.where(xh == 0, ga[:, :512], ga[:, 512:])
     gain_f = jnp.where(xh == 0, gf[:, :512], gf[:, 512:])
 
-    def emb_piece(s, t):
-        return r.emb[s, y, t, :, pl.ds(pl.multiple_of(xh * 512, 512), 512)].astype(F32)
+    def emb_piece(s, t, sub):
+        return r.emb[s, y, t, :, cols(sub)].astype(F32)
+
+    def halves(ref, zz, xx):
+        return jnp.concatenate([ref[zz, xx, h].reshape(ROWS, 512) for h in range(2)], axis=1)
+
+    def put(ref, zz, xx, v):
+        for h in range(2):
+            ref[zz, xx, h] = v[:, h * 512 : (h + 1) * 512].astype(BF).reshape(4, 3, 16, 512)
 
     def startup():
         for o in range(1, 8):
@@ -318,7 +319,7 @@
     first = {"w": True}
 
     def squares(s, g, zz, xx, which):
-        v = g[zz, xx].reshape(ROWS, 1024)
+        v = halves(g, zz, xx)
         gi_row = r.ginv[zz * 2 + xx, pl.ds(which, 1), :]
         acc = jnp.zeros((ROWS, 128), F32)
         for j in range(8):
@@ -329,16 +330,31 @@
     def stream(s):
         sends = []
         g, p = r.g.at[s], r.p.at[s]
-        fwd = [rest[t * 4].at[s] for t in range(3)]
-        land = [[rest[t * 4 + 1 + st].at[s] for st in range(3)] for t in range(3)]
-        for t in range(3):
-            own(g, t)[...] = (emb_piece(s, t) * gain_a).astype(BF)
-        it = gather(g, c, r.ag_s.at[s], r.ag_r.at[s])
-        next(it)
-        if s == 0:
-            startup()
-        yield
-        yield from it
+        fwd = [[rest[t * 4].at[s, sub] for t in range(3)] for sub in range(2)]
+        land = [[[rest[t * 4 + 1 + st].at[s, sub] for st in range(3)] for t in range(3)] for sub in range(2)]
+
+        def gathered(sub):
+            return gather(g, c, r.ag_s.at[s, sub], r.ag_r.at[s, sub], sub)
+
+        def scattered(sub):
+            return scatter(p, fwd[sub], land[sub], c, r.rs_s.at[s, sub], r.rs_r.at[s, sub], sub)
+
+        def through(sub):
+            drain(g, r.ag_s.at[s, sub], GATHERED)
+            yield from scattered(sub)
+            for t in range(3):
+                v = (emb_piece(s, t, sub) + own(p, t, sub)[...].astype(F32)).astype(BF)
+                r.res[s, sub, t] = v
+                own(g, t, sub)[...] = (v.astype(F32) * gain_f[:, sub * 256 : sub * 256 + 256]).astype(BF)
+            yield from gathered(sub)
+
+        for sub in range(2):
+            for t in range(3):
+                own(g, t, sub)[...] = (emb_piece(s, t, sub) * gain_a[:, sub * 256 : sub * 256 + 256]).astype(BF)
+        for step, _ in enumerate(in_turn(gathered(0), gathered(1))):
+            if s == 0 and step == STARTUP:
+                startup()
+            yield
 
         if first.pop("w", False):
             share_wait(1, r.wq)
@@ -351,7 +367,7 @@
 
         def qkv(i, carry):
             zz, xx = i // 2, i % 2
-            v = g[zz, xx].reshape(ROWS, 1024)
+            v = halves(g, zz, xx)
             wq = jnp.concatenate([r.wq[0, i], r.wq[1, i]], axis=1)
             q = mm(v, wq)
             r.acc[s, 0] += q[:, :128]
@@ -372,7 +388,7 @@
         tail = jnp.where(lane == 32, high, jnp.where(lane == 33, low, r.acc[s, 2]))
         sums = jnp.concatenate([r.acc[s, 0], r.acc[s, 1], tail], axis=1).astype(BF)
         r.qs[s] = mm(r.to_rows[...], sums).astype(BF).reshape(16, 16, 384)
-        for o in range(1, 16):
+        for o in FAR_FIRST:
             remote(r.qs.at[s, (col + o) % 16], r.qr.at[s, col], r.a2a_s.at[s, 0], r.a2a_r.at[s, 0], peer(o)).start()
         r.qr[s, col] = r.qs[s, col]
         yield
@@ -444,7 +460,7 @@
         ho = mm(r.by_head[...], o).astype(BF).reshape(8, 2, 16, 128)
         for h in range(8):
             r.ho[s, h] = jnp.concatenate([ho[h, 0], ho[h, 1]], axis=1)
-        for o_ in range(1, 16):
+        for o_ in FAR_FIRST:
             remote(
                 r.ho.at[s, ((col + o_) % 16) // 2], r.hr.at[s, col], r.a2a_s.at[s, 1], r.a2a_r.at[s, 1], peer(o_)
             ).start()
@@ -459,16 +475,11 @@
 
         def project(i, carry):
             w = jnp.concatenate([r.wo[0, i], r.wo[1, i]], axis=0)
-            p[i // 2, i % 2] = mm(attn, w).astype(BF).reshape(4, 3, 16, 1024)
+            put(p, i // 2, i % 2, mm(attn, w))
             return carry
 
         lax.fori_loop(0, 8, project, 0)
-        yield from scatter(p, fwd, land, c, r.rs_s.at[s], r.rs_r.at[s])
-        for t in range(3):
-            v = (emb_piece(s, t) + own(p, t)[...].astype(F32)).astype(BF)
-            r.res[s, t] = v
-            own(g, t)[...] = (v.astype(F32) * gain_f).astype(BF)
-        yield from gather(g, c, r.ag_s.at[s], r.ag_r.at[s])
+        yield from in_turn(through(0), through(1))
 
         if s == 0:
             share_wait(4, r.gate)
@@ -479,7 +490,7 @@
 
         def slab(i, carry):
             zz, xx = i // 2, i % 2
-            v = g[zz, xx].reshape(ROWS, 1024)
+            v = halves(g, zz, xx)
             for core in range(2):
                 w = jnp.concatenate([r.gate[core, i], gap, r.up[core, i], gap], axis=0)
                 v2 = mm_nt(v, w)
@@ -512,18 +523,21 @@
 
         def down(i, carry):
             v = mm(hidden, jnp.concatenate([r.wd[0, i], gap, r.wd[1, i], gap], axis=0))
-            p[i // 2, i % 2] = v.astype(BF).reshape(4, 3, 16, 1024)
+            put(p, i // 2, i % 2, v)
             return carry
 
+        for sub in range(2):
+            drain(p, r.rs_s.at[s, sub], SCATTERED)
         lax.fori_loop(0, 8, down, 0)
-        yield from scatter(p, fwd, land, c, r.rs_s.at[s], r.rs_r.at[s])
+        yield from in_turn(scattered(0), scattered(1))
 
         def fpiece(yy, hh):
             return r.fin.at[s, yy, :, :, pl.ds(pl.multiple_of(hh * 512, 512), 512)]
 
         for t in range(3):
-            v = r.res[s, t].astype(F32) + own(p, t)[...].astype(F32)
-            r.fin[s, y, t, :, pl.ds(pl.multiple_of(xh * 512, 512), 512)] = v.astype(BF)
+            for sub in range(2):
+                v = r.res[s, sub, t].astype(F32) + own(p, t, sub)[...].astype(F32)
+                r.fin[s, y, t, :, cols(sub)] = v.astype(BF)
         mine = fpiece(y, xh)
 
         def fsend(piece, target, i):
@@ -534,13 +548,13 @@
         def farrive(piece, i):
             remote(piece, piece, r.f_s.at[s, i], r.f_r.at[s, i], mate).wait_recv()
 
+        theirs = fpiece(y, 1 - xh)
         fsend(mine, device(far), 0)
-        for o_ in (1, 3, 2):
+        for o_ in (2, 1, 3):
             fsend(mine, device(moved(c, "y", o_)), o_)
         yield
-        theirs = fpiece(y, 1 - xh)
         farrive(theirs, 0)
-        for o_ in (1, 3, 2):
+        for o_ in (2, 1, 3):
             fsend(theirs, device(moved(c, "y", o_)), 3 + o_)
         yield
         for o_ in (1, 2, 3):
@@ -551,13 +565,16 @@
         cp.start()
         for e in sends:
             e.wait_send()
+        for sub in range(2):
+            drain(g, r.ag_s.at[s, sub], GATHERED)
+            drain(p, r.rs_s.at[s, sub], SCATTERED)
         for i, ref in ((0, r.qr), (1, r.hr)):
             part = ref.at[s, pl.ds(0, 15)]
             pltpu.make_async_copy(part, part, r.a2a_s.at[s, i]).wait()
         cp.wait()
 
     live = [stream(s) for s in range(STEPS)]
-    for s in SCHEDULE:
+    for s in "".join(SCHEDULE):
         next(live[int(s)], None)
     for it in live:
         for _ in it:
@@ -568,7 +585,18 @@
         pair[i].wait_send()
 
 
-SCHEDULE = "0101001" + "01" * 22
+STARTUP = 3
+SCHEDULE = (
+    "0101001000011001110110010001001100110011001101",
+    "1001110101001100111010110011010101100110011100",
+)
+
+
+def finish(out_in, app_in, out, app):
+    out[...] = out_in[...]
+    for s in range(STEPS):
+        both = [app_in[s, i].astype(F32)[:LOCAL].reshape(LOCAL, 1, HEAD) for i in range(2)]
+        app[s] = jnp.concatenate(both, axis=1).astype(BF)
 
 
 def rope_frequency(head_size):
@@ -598,8 +626,8 @@
     vmem = pl.BlockSpec(memory_space=pltpu.VMEM)
     smem = pl.BlockSpec(memory_space=pltpu.SMEM)
     scratch = [
-        pltpu.VMEM((2, 4, 2, 4, 3, 16, 1024), BF),
-        pltpu.VMEM((2, 4, 2, 4, 3, 16, 1024), BF),
+        pltpu.VMEM((2, 4, 2, 2, 4, 3, 16, 512), BF),
+        pltpu.VMEM((2, 4, 2, 2, 4, 3, 16, 512), BF),
         pltpu.VMEM((2, 4, 3, 16, 1024), BF),
         pltpu.VMEM((2, 8, 1024, 128), BF),
         pltpu.VMEM((2, 2, 8, 8, 1024), BF),
@@ -623,7 +651,7 @@
         pltpu.VMEM((2, 16, 16, 256), BF),
         pltpu.VMEM((2, 4, ROWS, 128), F32),
         pltpu.VMEM((2, 4, ROWS, 128), F32),
-        pltpu.VMEM((2, 3, 16, 512), BF),
+        pltpu.VMEM((2, 2, 3, 16, 256), BF),
         pltpu.VMEM((2, 4, 3, 16, 1024), BF),
         pltpu.VMEM((256, ROWS), BF),
         pltpu.VMEM((ROWS, 256), BF),
@@ -635,10 +663,10 @@
         pltpu.SemaphoreType.DMA((2,)),
         pltpu.SemaphoreType.DMA((10,)),
         pltpu.SemaphoreType.DMA((10,)),
-        pltpu.SemaphoreType.DMA((2, 3)),
-        pltpu.SemaphoreType.DMA((2, 9)),
-        pltpu.SemaphoreType.DMA((2, 3)),
-        pltpu.SemaphoreType.DMA((2, 9)),
+        pltpu.SemaphoreType.DMA((2, 2, 3)),
+        pltpu.SemaphoreType.DMA((2, 2, 9)),
+        pltpu.SemaphoreType.DMA((2, 2, 3)),
+        pltpu.SemaphoreType.DMA((2, 2, 9)),
         pltpu.SemaphoreType.DMA((2, 2)),
         pltpu.SemaphoreType.DMA((2, 2)),
         pltpu.SemaphoreType.DMA((1,)),
@@ -650,10 +678,10 @@
     ]
     for t in range(3):
         full = ORDERS[t][:2]
-        scratch.append(pltpu.VMEM((2, 2) + lead_shape(full) + (16, width_of(full) // 2), BF))
+        scratch.append(pltpu.VMEM((2, 2, 2) + lead_shape(full) + (16, 128), BF))
         for st in range(3):
             full = ORDERS[t][: 2 - st]
-            scratch.append(pltpu.VMEM((2, 3 if st else 2) + lead_shape(full) + (16, width_of(full)), BF))
+            scratch.append(pltpu.VMEM((2, 2, 3 if st else 2) + lead_shape(full) + (16, 256), BF))
     out, app = pl.pallas_call(
         kernel,
         out_shape=(
@@ -683,7 +711,15 @@
         positions,
         freq,
     )
-    return out.reshape(2, ROWS, 1024), app[:, :, :LOCAL].transpose(0, 2, 1, 3)
+    return pl.pallas_call(
+        finish,
+        out_shape=(
+            jax.ShapeDtypeStruct((2, ROWS, 1024), BF),
+            jax.ShapeDtypeStruct((2, LOCAL, 2, HEAD), BF),
+        ),
+        in_specs=[vmem, vmem],
+        out_specs=(vmem, vmem),
+    )(out.reshape(2, ROWS, 1024), app)
 
 
 def solution(mesh):

time: 162 us -> 151 us (0.932)
  Pallas kernels: 157 us -> 150 us
  local copies, waits for them, and re-layouts: 3.39 us -> 0 us
    pallas_call x1, Pallas kernels: 157 us -> 148 us  [on_device(): pl.pallas_call(kernel, out_shape=(jax.ShapeDtypeStruct((2, 4, 3, 16, 1024...]
    unnamed x2 -> x0, local copies, waits for them, and re-layouts: 2.67 us -> none
    pallas_call x0 -> x1, Pallas kernels: none -> 2.07 us  [on_device(): pl.pallas_call(finish, out_shape=(jax.ShapeDtypeStruct((2, ROWS, 1024), B...]
where the time goes in v2:
time: 151 us
  Pallas kernels  150 us (99%)
    pallas_call x1, Pallas kernels, on_device(): pl.pallas_call(kernel, out_shape=(jax.ShapeDtypeStruct((2, 4, 3, 16, 1024...  148 us

profile of v2, /device:TPU:0, one launch (start us, length us, event | category | flops | bytes accessed | tf_op | source)
XLA Modules:
  0.0 151.1 jit_solution(8564083391759965116)
XLA Ops:
  0.6 0.6 maximum_bitcast_fusion.refs_14_
  1.2 147.8 %shard_map.149 = (bf16[2,4,3,16,1024]{4,3,2,1,0:T(8,128)(2,1)}, bf16[2,2,16,128]{3,2,1,0:T(8,128)(2,1)}) custom-call(bf16[2,4,3,16,1024]{4,3,2,1,0:T(8,128)(2,1)} %bitcast.16, bf16[1024]{0:T(1024)(128)(2,1)} %refs_1_.1, bf16[1024]{0:T(1024)(128)(2,1)} %refs_2_.1, bf16[8,2,1024,128]{3,2,1,0:T(8,128)(2,1)} %bitcast.11, bf16[8,16384]{1,0:T(8,128)(2,1)} %bitcast.18, ...), custom_call_target="tpu_custom_call" | custom-call | tf_op jit(solution)/shard_map/pallas_call | solution.py:685
  149.0 2.1 %shard_map.150 = (bf16[2,192,1024]{2,1,0:T(8,128)(2,1)}, bf16[2,12,2,128]{3,2,1,0:T(2,128)(2,1)}) custom-call(bf16[2,192,1024]{2,1,0:T(8,128)(2,1)} %bitcast.17, bf16[2,2,16,128]{3,2,1,0:T(8,128)(2,1)} %get-tuple-element.5.app_in), custom_call_target="tpu_custom_call" | custom-call | tf_op jit(solution)/shard_map/pallas_call | solution.py:714
  (1 shorter events, 0.0 us)

commit v3 on v2

--- a/solution.py
+++ b/solution.py
@@ -585,7 +585,7 @@
         pair[i].wait_send()
 
 
-STARTUP = 3
+STARTUP = 1
 SCHEDULE = (
     "0101001000011001110110010001001100110011001101",
     "1001110101001100111010110011010101100110011100",

time: 151 us -> 150 us (level)
  Pallas kernels: 150 us -> 148 us
    pallas_call x1, Pallas kernels: 148 us -> 146 us  [on_device(): pl.pallas_call(kernel, out_shape=(jax.ShapeDtypeStruct((2, 4, 3, 16, 1024...]
where the time goes in v3:
time: 150 us; the launch traced here: 149 us
  Pallas kernels  148 us (99%)
    pallas_call x1, Pallas kernels, on_device(): pl.pallas_call(kernel, out_shape=(jax.ShapeDtypeStruct((2, 4, 3, 16, 1024...  146 us

profile of v3, /device:TPU:0, one launch (start us, length us, event | category | flops | bytes accessed | tf_op | source)
XLA Modules:
  0.0 149.4 jit_solution(16602034796672590189)
XLA Ops:
  0.6 0.6 maximum_bitcast_fusion.refs_14_
  1.2 146.1 %shard_map.149 = (bf16[2,4,3,16,1024]{4,3,2,1,0:T(8,128)(2,1)}, bf16[2,2,16,128]{3,2,1,0:T(8,128)(2,1)}) custom-call(bf16[2,4,3,16,1024]{4,3,2,1,0:T(8,128)(2,1)} %bitcast.16, bf16[1024]{0:T(1024)(128)(2,1)} %refs_1_.1, bf16[1024]{0:T(1024)(128)(2,1)} %refs_2_.1, bf16[8,2,1024,128]{3,2,1,0:T(8,128)(2,1)} %bitcast.11, bf16[8,16384]{1,0:T(8,128)(2,1)} %bitcast.18, ...), custom_call_target="tpu_custom_call" | custom-call | tf_op jit(solution)/shard_map/pallas_call | solution.py:685
  147.4 2.1 %shard_map.150 = (bf16[2,192,1024]{2,1,0:T(8,128)(2,1)}, bf16[2,12,2,128]{3,2,1,0:T(2,128)(2,1)}) custom-call(bf16[2,192,1024]{2,1,0:T(8,128)(2,1)} %bitcast.17, bf16[2,2,16,128]{3,2,1,0:T(8,128)(2,1)} %get-tuple-element.5.app_in), custom_call_target="tpu_custom_call" | custom-call | tf_op jit(solution)/shard_map/pallas_call | solution.py:714
  (1 shorter events, 0.0 us)
